TPU v7x, 32 devices: a whole 2x2x4 slice. The times are simulated.
32 devices in a mesh: dp: 8 (over z, x), zero: 4 (over y, core).
Axes of the slice: x: 2, y: 2, z: 4, core: 2. Of those that a mesh axis runs over, the one named last changes fastest.
Arguments:
- grad_parts: bfloat16 [8, 3, 704, 1024], P('dp', None, 'zero'), may hold values from -1.5 to 1.5
- momentum: float32 [3, 704, 1024], P(None, 'zero')
- owner_table: int32 [3], replicated, may hold values from 0 to 3, as said below
Outputs:
- new_momentum: float32 [3, 704, 1024], P(None, 'zero')
- update: bfloat16 [3, 704, 1024], P(None, 'zero')
- owner_copy: bfloat16 [4, 704, 1024], P('zero')
Inputs may be any that keep to these rules, and one draw needn't show every extreme that they name: `owner_table`: the 3 entries are distinct; the first and the last device along zero always own a matrix.
All inputs are finite; a program needn't handle non-finite values.
Results may differ from a plain program's by a relative error of at most 0.0062.
Values may be sent and summed in bfloat16 or wider, within the bound.
A program may use at most 64 MiB of HBM per device.

v0:
```python
import math

import jax
import jax.numpy as jnp
from jax import lax
from jax.sharding import PartitionSpec as P

D = 1024
ITERS = 2


COEF_A = 3.4445
COEF_B = -4.775
COEF_C = 2.0315
MOMENTUM_DECAY = 0.95
NORM_EPSILON = 1e-07


def orthogonalize(matrix):
    current = matrix
    iterate = matrix.astype(jnp.float32)
    for step in range(ITERS):
        gram_matrix = jnp.dot(current, current.T, preferred_element_type=jnp.float32).astype(
            jnp.bfloat16
        )
        squared = jnp.dot(gram_matrix, gram_matrix, preferred_element_type=jnp.float32)
        poly_term = (COEF_B * gram_matrix.astype(jnp.float32) + COEF_C * squared).astype(
            jnp.bfloat16
        )
        iterate = COEF_A * current.astype(jnp.float32) + jnp.dot(
            poly_term, current, preferred_element_type=jnp.float32
        )
        if step + 1 < ITERS:
            current = iterate.astype(jnp.bfloat16)
    return (0.2 * math.sqrt(D) * iterate).astype(jnp.bfloat16)


def on_device(grad_parts, momentum, owner_table):
    my_index = lax.axis_index("zero")
    local_part = grad_parts[0].astype(jnp.float32)
    summed = lax.psum(local_part, "dp")
    new_momentum = MOMENTUM_DECAY * momentum + summed
    partial_value = jnp.sum(new_momentum * new_momentum, axis=(1, 2))
    squares = lax.psum(partial_value, "zero")
    inverse = 1.0 / (jnp.sqrt(squares) + NORM_EPSILON)
    start_rows = (new_momentum * inverse[:, None, None]).astype(jnp.bfloat16)
    mine_mask = (owner_table == my_index).astype(jnp.bfloat16)
    gathered = lax.all_gather(start_rows, "zero", axis=1, tiled=True)
    full_matrix = jnp.einsum(
        "j,jrd->rd", mine_mask, gathered, preferred_element_type=jnp.float32
    ).astype(jnp.bfloat16)
    result = orthogonalize(full_matrix)
    contrib = mine_mask.astype(jnp.float32)[:, None, None] * result.astype(jnp.float32)[None]
    update_rows = lax.psum_scatter(
        contrib.astype(jnp.bfloat16), "zero", scatter_dimension=1, tiled=True
    )
    return (new_momentum, update_rows, result[None])


def solution(mesh):
    placed = (P("dp", None, "zero", None), P(None, "zero", None), P())
    return jax.shard_map(
        on_device,
        mesh=mesh,
        in_specs=placed,
        out_specs=(P(None, "zero", None), P(None, "zero", None), P("zero", None, None)),
        check_vma=False,
    )
```

profile of v0, /device:TPU:0, one launch (start us, length us, event | category | flops | bytes accessed | tf_op | source)
XLA Modules:
  0.0 243.4 jit_solution(9624275397225432035)
XLA Ops:
  7.2 0.0 all-reduce.2.cloned.1.call-start
  7.2 2.8 %bitcast_convert_fusion.1 = f32[3,176,1024]{2,1,0:T(8,128)} fusion(bf16[1,3,176,1024]{3,2,1,0:T(8,128)(2,1)} %param.3), kind=kLoop, calls=%fused_computation.13 | loop fusion | flops 540672 | bytes 3244032 | tf_op jit(solution)/shard_map/convert_element_type | solution.py:40
  10.0 0.0 all-reduce.2.cloned.1.call-update
  10.1 0.0 all-gather.2.cloned.1.call-start
  10.1 107.7 %all-reduce.2.cloned.1.call-done = f32[3,176,1024]{2,1,0:T(8,128)} async-done(((f32[3,176,1024]{2,1,0:T(8,128)}), f32[3,176,1024]{2,1,0:T(8,128)}) %all-reduce.2.cloned.1.call-update) | async-done | bytes 2162704 | tf_op jit(solution)/shard_map/psum | solution.py:41
  117.9 2.8 %multiply_reduce_fusion = (f32[3]{0:T(128)S(1)}, f32[3,176,1024]{2,1,0:T(8,128)S(1)}) fusion(f32[3,176,1024]{2,1,0:T(8,128)} %all-reduce.2.cloned.1.call-done, f32[3,176,1024]{2,1,0:T(8,128)} %param.4), kind=kLoop, calls=%fused_computation.9 | loop fusion | flops 2162685 | bytes 6488076 | tf_op jit(solution)/shard_map/reduce_sum | solution.py:43
  120.7 0.0 copy-start
  120.7 6.3 %psum.15 = f32[3]{0:T(128)S(1)} all-reduce(f32[3]{0:T(128)S(1)} %get-tuple-element.3), channel_id=1, replica_groups=mesh['dp'=8,'zero'=4] {'zero'}, use_global_device_ids=true, to_apply=%region_2.0 | all-reduce | flops 3 | bytes 24 | tf_op jit(solution)/shard_map/psum | solution.py:44
  127.0 0.0 copy-start.1
  127.0 1.3 multiply_convert_fusion.2
  128.3 0.0 all-gather.2.cloned.1.call-update
  128.3 0.0 copy-done
  128.3 0.0 reduce-scatter.2.cloned.1.call-start
  128.4 0.0 copy-done.1
  128.4 34.7 %all-gather.2.cloned.1.call-done = bf16[3,704,1024]{2,1,0:T(8,128)(2,1)} async-done(((bf16[3,176,1024]{2,1,0:T(8,128)(2,1)}), bf16[3,704,1024]{2,1,0:T(8,128)(2,1)}) %all-gather.2.cloned.1.call-update) | async-done | bytes 4325392 | tf_op jit(solution)/shard_map/all_gather | solution.py:48
  163.1 6.0 %fusion = bf16[1,704,1024]{2,0,1:T(2,128)(2,1)S(1)} fusion(bf16[3,704,1024]{2,1,0:T(8,128)(2,1)} %all-gather.2.cloned.1.call-done, s32[3]{0:T(128)S(1)} %copy-done.1, s32[]{:T(128)S(6)} %axis_index.12), kind=kOutput, calls=%fused_computation.1 | convolution fusion | flops 4325379 | bytes 5767184 | tf_op jit(solution)/shard_map/j,jrd->rd/dot_general | solution.py:49
  169.2 2.5 %convolution_convert_fusion.1 = bf16[704,704]{1,0:T(8,128)(2,1)} fusion(bf16[1,704,1024]{2,0,1:T(2,128)(2,1)S(1)} %fusion), kind=kOutput, calls=%fused_computation.12 | convolution fusion | flops 1015517184 | bytes 2433024 | tf_op jit(solution)/shard_map/dot_general | solution.py:23
  171.7 5.9 %add_convert_fusion = bf16[704,1024]{1,0:T(8,128)(2,1)} fusion(bf16[704,704]{1,0:T(8,128)(2,1)} %convolution_convert_fusion.1, bf16[1,704,1024]{2,0,1:T(2,128)(2,1)S(1)} %fusion), kind=kOutput, calls=%fused_computation.5 | convolution fusion | flops 1718210560 | bytes 3874816 | tf_op jit(solution)/shard_map/dot_general | solution.py:30
  177.6 4.1 %convolution_convert_fusion = bf16[704,704]{1,0:T(8,128)(2,1)} fusion(bf16[704,1024]{1,0:T(8,128)(2,1)} %add_convert_fusion), kind=kOutput, calls=%fused_computation.11 | convolution fusion | flops 1015517184 | bytes 2433024 | tf_op jit(solution)/shard_map/dot_general | solution.py:23
  181.7 6.4 %fusion.10 = (f32[704,1024]{1,0:T(8,128)S(1)}, bf16[704,1024]{1,0:T(8,128)(2,1)}) fusion(bf16[704,1024]{1,0:T(8,128)(2,1)} %add_convert_fusion, bf16[704,704]{1,0:T(8,128)(2,1)} %convolution_convert_fusion), kind=kOutput, calls=%fused_computation.24 | convolution fusion | flops 1719652352 | bytes 6758400 | tf_op jit(solution)/shard_map/dot_general | solution.py:30
  188.1 3.2 %multiply_convert_fusion = bf16[3,704,1024]{2,1,0:T(8,128)(2,1)} fusion(f32[704,1024]{1,0:T(8,128)S(1)} %get-tuple-element.5, f32[3]{0:T(128)S(1)} %fusion.4), kind=kLoop, calls=%fused_computation | loop fusion | flops 4325376 | bytes 7208972 | tf_op jit(solution)/shard_map/convert_element_type | solution.py:55
  191.3 0.0 reduce-scatter.2.cloned.1.call-update
  191.4 45.5 %reduce-scatter.2.cloned.1.call-done = bf16[3,176,1024]{2,1,0:T(8,128)(2,1)} async-done(((bf16[3,704,1024]{2,1,0:T(8,128)(2,1)}), bf16[3,176,1024]{2,1,0:T(8,128)(2,1)}) %reduce-scatter.2.cloned.1.call-update) | async-done | bytes 1081360 | tf_op jit(solution)/shard_map/reduce_scatter | solution.py:54
  (2 shorter events, 0.0 us)
Async XLA Ops:
  7.2 110.7 %all-reduce.2.cloned.1.call-start = ((), (), s32[]{:S(2)}) async-start(), calls=%async_computation.1 | async-start | bytes 4325376 | tf_op jit(solution)/shard_map/psum | solution.py:41
  10.1 153.0 %all-gather.2.cloned.1.call-start = ((), (), s32[]{:S(2)}) async-start(), calls=%async_computation.2 | async-start | bytes 5406720 | tf_op jit(solution)/shard_map/all_gather | solution.py:48
  120.7 7.6 %copy-start = (f32[3,176,1024]{2,1,0:T(8,128)}, f32[3,176,1024]{2,1,0:T(8,128)S(1)}, u32[]{:S(2)}) copy-start(f32[3,176,1024]{2,1,0:T(8,128)S(1)} %get-tuple-element.4) | copy-start | bytes 6488068
  127.0 1.4 copy-start.1
  128.3 108.5 %reduce-scatter.2.cloned.1.call-start = ((), (), s32[]{:S(2)}) async-start(), calls=%async_computation.3 | async-start | bytes 5406720 | tf_op jit(solution)/shard_map/reduce_scatter | solution.py:54
Sparse Core Ops, SparseCore 0:
  12.2 105.6 all-reduce.1
  128.4 34.6 all-gather.1
  191.5 45.3 reduce-scatter.1
where the time goes:
time: 244 us; the launch traced here: 243 us
  waiting for transfers between devices  188 us (77%)
  matrix products  25 us (10%)
  between operations  13.8 us (6%)
  other arithmetic  10.2 us (4%)
  blocking collectives  6.29 us (3%)
    psum x1, waiting for transfers between devices, on_device(): summed = lax.psum(local_part, 'dp')  108 us
    reduce_scatter x1, waiting for transfers between devices, on_device(): lax.psum_scatter(contrib.astype(jnp.bfloat16), 'zero', scatter_dimension=...  45.5 us
    all_gather x1, waiting for transfers between devices, on_device(): gathered = lax.all_gather(start_rows, 'zero', axis=1, tiled=True)  34.7 us
    dot_general x2, matrix products, orthogonalize(): jnp.dot(poly_term, current, preferred_element_type=jnp.float32)  12.3 us
    dot_general x2, matrix products, orthogonalize(): jnp.dot(current, current.T, preferred_element_type=jnp.float32)  6.65 us
    psum x1, blocking collectives, on_device(): squares = lax.psum(partial_value, 'zero')  6.29 us
    dot_general x1, matrix products, on_device(): jnp.einsum('j,jrd->rd', mine_mask, gathered, preferred_element_type=jnp.f...  6.04 us
  transfers between devices with their start and end apart: 3, of which 3 were waited for; matrix products, arithmetic and copies ran while one was open for 0% of the time, Pallas kernels for 0%

commit v1 on v0

--- a/solution.py
+++ b/solution.py
@@ -3,17 +3,18 @@
 import jax
 import jax.numpy as jnp
 from jax import lax
+from jax.experimental import pallas as pl
+from jax.experimental.pallas import tpu as pltpu
 from jax.sharding import PartitionSpec as P
 
-D = 1024
 ITERS = 2
-
-
 COEF_A = 3.4445
 COEF_B = -4.775
 COEF_C = 2.0315
 MOMENTUM_DECAY = 0.95
 NORM_EPSILON = 1e-07
+MESH = pl.DeviceIdType.MESH
+LANES = 128
 
 
 def orthogonalize(matrix):
@@ -32,10 +33,10 @@
         )
         if step + 1 < ITERS:
             current = iterate.astype(jnp.bfloat16)
-    return (0.2 * math.sqrt(D) * iterate).astype(jnp.bfloat16)
-
-
-def on_device(grad_parts, momentum, owner_table):
+    return (0.2 * math.sqrt(matrix.shape[1]) * iterate).astype(jnp.bfloat16)
+
+
+def general_step(grad_parts, momentum, owner_table):
     my_index = lax.axis_index("zero")
     local_part = grad_parts[0].astype(jnp.float32)
     summed = lax.psum(local_part, "dp")
@@ -57,7 +58,299 @@
     return (new_momentum, update_rows, result[None])
 
 
+def column_tiles(width, step=256):
+    return [(at, min(step, width - at)) for at in range(0, width, step)]
+
+
+def make_kernel(n_dp, n_zero, mats, rows, dim):
+    hid = rows * n_zero
+    n_line = n_dp // 2
+    width = dim // n_dp
+    out_scale = 0.2 * math.sqrt(dim)
+
+    def kernel(
+        grad, momentum, nm_out, up_out,
+        x, parts, mom, gram, poly, scale,
+        rs_s, rs_r, s1_s, s1_r, s2_s, s2_r, s3_s, s3_r, s4_s, s4_r, local,
+    ):
+        d = lax.axis_index("dp")
+        o = lax.axis_index("zero")
+        zi, xi, yi, ci = d // 2, d % 2, o // 2, o % 2
+        x_peer = zi * 2 + 1 - xi
+        y_peer = (1 - yi) * 2 + ci
+        c_peer = yi * 2 + 1 - ci
+
+        def row(s):
+            return pl.ds(pl.multiple_of(s * rows, 16), rows)
+
+        def col(k):
+            return pl.ds(pl.multiple_of(k * width, LANES), width)
+
+        def chunk(j, s, k):
+            return x.at[j, row(s), col(k)]
+
+        def line(r):
+            return (zi + n_line - r) % n_line
+
+        def remote(src, dst, send, recv, to):
+            return pltpu.make_async_remote_copy(
+                src_ref=src, dst_ref=dst, send_sem=send, recv_sem=recv,
+                device_id=to, device_id_type=MESH,
+            )
+
+        def rs(j, r):
+            p = (d + r) % n_dp
+            return remote(grad.at[0, j, :, col(p)], parts.at[j, r], rs_s.at[j, r], rs_r.at[j, r], (p, o))
+
+        def s1(j, r):
+            c = chunk(j, o, d)
+            return remote(c, c, s1_s.at[j, r], s1_r.at[j, r], (((zi + r) % n_line) * 2 + xi, o))
+
+        def s1_in(j, r):
+            c = chunk(j, o, line(r) * 2 + xi)
+            return remote(c, c, s1_s.at[j, r], s1_r.at[j, r], (((zi + r) % n_line) * 2 + xi, o))
+
+        def s2(j, r):
+            c = chunk(j, o, line(r) * 2 + xi)
+            return remote(c, c, s2_s.at[j, r], s2_r.at[j, r], (x_peer, o))
+
+        def s2_in(j, r):
+            c = chunk(j, o, line(r) * 2 + 1 - xi)
+            return remote(c, c, s2_s.at[j, r], s2_r.at[j, r], (x_peer, o))
+
+        def s3(j, r, h, s=None):
+            k = line(r) * 2 + (xi if h == 0 else 1 - xi)
+            c = chunk(j, o if s is None else s, k)
+            return remote(c, c, s3_s.at[j, r, h], s3_r.at[j, r, h], (d, y_peer))
+
+        def s3_in(j, r, h):
+            return s3(j, r, h, y_peer)
+
+        def s4(j, h, s=None):
+            if s is None:
+                s = o if h == 0 else y_peer
+            c = x.at[j, row(s), :]
+            return remote(c, c, s4_s.at[j, h], s4_r.at[j, h], (d, c_peer))
+
+        def s4_in(j, h):
+            return s4(j, h, c_peer if h == 0 else (1 - yi) * 2 + 1 - ci)
+
+        def own_part(j):
+            return pltpu.make_async_copy(grad.at[0, j, :, col(d)], parts.at[j, 0], local.at[j])
+
+        def own_momentum():
+            return pltpu.make_async_copy(momentum.at[:, :, col(d)], mom, local.at[mats])
+
+        def nm_copy(j):
+            return pltpu.make_async_copy(x.at[j, row(o), :], nm_out.at[j], local.at[mats + 1 + j])
+
+        def up_copy(j):
+            return pltpu.make_async_copy(x.at[j], up_out.at[j], local.at[2 * mats + 1 + j])
+
+        peers = [((d + r) % n_dp, o) for r in range(1, n_dp)] + [(d, y_peer), (d, c_peer)]
+        barrier = pltpu.get_barrier_semaphore()
+        own_momentum().start()
+        for j in range(mats):
+            own_part(j).start()
+        for to in peers:
+            pl.semaphore_signal(barrier, inc=1, device_id=to, device_id_type=MESH)
+        pl.semaphore_wait(barrier, len(peers))
+        for j in range(mats):
+            for r in range(1, n_dp):
+                rs(j, r).start()
+
+        def phase_a(j):
+            if j == 0:
+                own_momentum().wait()
+            own_part(j).wait()
+            for r in range(1, n_dp):
+                rs(j, r).wait_recv()
+            total = parts[j, 0].astype(jnp.float32)
+            for r in range(1, n_dp):
+                total = total + parts[j, r].astype(jnp.float32)
+            x[j, row(o), col(d)] = (MOMENTUM_DECAY * mom[j] + total).astype(jnp.bfloat16)
+            s3(j, 0, 0).start()
+            s2(j, 0).start()
+            for r in range(1, n_line):
+                s1(j, r).start()
+
+        def phase_b(j):
+            for r in range(1, n_line):
+                s1_in(j, r).wait_recv()
+                s2(j, r).start()
+                s3(j, r, 0).start()
+
+        def phase_c(j):
+            for r in range(n_line):
+                s2_in(j, r).wait_recv()
+                s3(j, r, 1).start()
+            s4(j, 0).start()
+            nm_copy(j).start()
+
+        def phase_d(j):
+            for r in range(n_line):
+                for h in range(2):
+                    s3_in(j, r, h).wait_recv()
+            s4(j, 1).start()
+
+        def phase_e(j):
+            for h in range(2):
+                s4_in(j, h).wait_recv()
+            for r in range(1, n_dp):
+                rs(j, r).wait_send()
+            for r in range(1, n_line):
+                s1(j, r).wait_send()
+            for r in range(n_line):
+                s2(j, r).wait_send()
+                for h in range(2):
+                    s3(j, r, h).wait_send()
+            for h in range(2):
+                s4(j, h).wait_send()
+            nm_copy(j).wait()
+
+        def ns_step(t):
+            j, it = t // ITERS, t % ITERS
+
+            @pl.when(it == 0)
+            def _():
+                def add(i, acc):
+                    v = x[j, pl.ds(pl.multiple_of(i * 16, 16), 16), :].astype(jnp.float32)
+                    return acc + v * v
+
+                acc = lax.fori_loop(0, hid // 16, add, jnp.zeros((16, dim), jnp.float32))
+                total = jnp.sum(jnp.sum(acc, axis=0, keepdims=True), axis=1, keepdims=True)
+                scale[...] = jnp.broadcast_to(1.0 / (jnp.sqrt(total) + NORM_EPSILON), scale.shape)
+
+            @pl.when(it != 0)
+            def _():
+                scale[...] = jnp.ones(scale.shape, jnp.float32)
+
+            s = scale[0:1, 0:1]
+            for at, size in column_tiles(hid):
+                g = lax.dot_general(
+                    x[j], x[j, at : at + size, :], (((1,), (1,)), ((), ())),
+                    preferred_element_type=jnp.float32,
+                )
+                gram[:, at : at + size] = (g * s * s).astype(jnp.bfloat16)
+            for at, size in column_tiles(hid):
+                block = gram[:, at : at + size]
+                q = jnp.dot(gram[...], block, preferred_element_type=jnp.float32)
+                poly[:, at : at + size] = (COEF_B * block.astype(jnp.float32) + COEF_C * q).astype(
+                    jnp.bfloat16
+                )
+            last = (it == ITERS - 1).astype(jnp.float32)
+            post = s * (1.0 + last * (out_scale - 1.0))
+
+            def apply(i, carry):
+                cols = pl.ds(pl.multiple_of(i * 256, 256), 256)
+                block = x[j, :, cols]
+                y = COEF_A * block.astype(jnp.float32) + jnp.dot(
+                    poly[...], block, preferred_element_type=jnp.float32
+                )
+                x[j, :, cols] = (y * post).astype(jnp.bfloat16)
+                return carry
+
+            lax.fori_loop(0, dim // 256, apply, 0)
+
+        phase_a(0)
+        phase_b(0)
+        phase_c(0)
+        phase_a(1)
+        phase_d(0)
+        phase_b(1)
+        phase_c(1)
+        phase_e(0)
+
+        def step(t, carry):
+            ns_step(t)
+
+            @pl.when(t == 0)
+            def _():
+                phase_a(2)
+                phase_b(2)
+
+            @pl.when(t == 1)
+            def _():
+                up_copy(0).start()
+                phase_c(2)
+                phase_d(1)
+                phase_e(1)
+
+            @pl.when(t == 2)
+            def _():
+                phase_d(2)
+
+            @pl.when(t == 3)
+            def _():
+                up_copy(1).start()
+                phase_e(2)
+
+            return carry
+
+        lax.fori_loop(0, mats * ITERS, step, 0)
+        up_copy(2).start()
+        for j in range(mats):
+            up_copy(j).wait()
+
+    dma = pltpu.SemaphoreType.DMA
+    flops = mats * ITERS * 2 * hid * hid * (2 * dim + hid)
+    return pl.pallas_call(
+        kernel,
+        out_shape=(
+            jax.ShapeDtypeStruct((mats, rows, dim), jnp.bfloat16),
+            jax.ShapeDtypeStruct((mats, hid, dim), jnp.bfloat16),
+        ),
+        in_specs=[pl.BlockSpec(memory_space=pl.ANY)] * 2,
+        out_specs=(pl.BlockSpec(memory_space=pl.ANY),) * 2,
+        scratch_shapes=[
+            pltpu.VMEM((mats, hid, dim), jnp.bfloat16),
+            pltpu.VMEM((mats, n_dp, rows, width), jnp.bfloat16),
+            pltpu.VMEM((mats, rows, width), jnp.float32),
+            pltpu.VMEM((hid, hid), jnp.bfloat16),
+            pltpu.VMEM((hid, hid), jnp.bfloat16),
+            pltpu.VMEM((8, LANES), jnp.float32),
+            dma((mats, n_dp)), dma((mats, n_dp)),
+            dma((mats, n_line)), dma((mats, n_line)),
+            dma((mats, n_line)), dma((mats, n_line)),
+            dma((mats, n_line, 2)), dma((mats, n_line, 2)),
+            dma((mats, 2)), dma((mats, 2)),
+            dma((3 * mats + 1,)),
+        ],
+        cost_estimate=pl.CostEstimate(flops=flops, bytes_accessed=16 * mats * rows * dim, transcendentals=0),
+        compiler_params=pltpu.CompilerParams(
+            collective_id=0, has_side_effects=True, vmem_limit_bytes=40 * 1024 * 1024
+        ),
+    )
+
+
 def solution(mesh):
+    n_dp, n_zero = mesh.shape["dp"], mesh.shape["zero"]
+
+    def kernel_step(grad_parts, momentum, owner_table):
+        _, mats, rows, dim = grad_parts.shape
+        me = lax.axis_index("zero")
+        nm, update = make_kernel(n_dp, n_zero, mats, rows, dim)(grad_parts, momentum)
+        mine = owner_table == me
+        which = jnp.argmax(mine)
+        copy = lax.dynamic_index_in_dim(update, which, 0, keepdims=True)
+        copy = jnp.where(jnp.any(mine), copy, jnp.zeros_like(copy))
+        update_rows = lax.dynamic_slice_in_dim(update, me * rows, rows, axis=1)
+        return nm.astype(jnp.float32), update_rows, copy
+
+    def on_device(grad_parts, momentum, owner_table):
+        _, mats, rows, dim = grad_parts.shape
+        fits = (
+            mats == 3
+            and n_zero == 4
+            and n_dp % 2 == 0
+            and n_dp >= 4
+            and dim % (LANES * n_dp) == 0
+            and dim % 256 == 0
+            and rows % 16 == 0
+        )
+        body = kernel_step if fits else general_step
+        return body(grad_parts, momentum, owner_table)
+
     placed = (P("dp", None, "zero", None), P(None, "zero", None), P())
     return jax.shard_map(
         on_device,

time: 244 us -> 97.2 us (0.40)
  waiting for transfers between devices: 188 us -> 0 us
  Pallas kernels: 0 us -> 82.5 us
  matrix products: 25 us -> 0 us
  between operations: 13.8 us -> 2.61 us
  local copies, waits for them, and re-layouts: 0.01 us -> 6.32 us
  blocking collectives: 6.29 us -> 0 us
  other arithmetic: 10.2 us -> 5.52 us
    psum x1 -> x0, waiting for transfers between devices: 108 us -> none  [on_device(): summed = lax.psum(local_part, 'dp')]
    pallas_call x0 -> x1, Pallas kernels: none -> 82.5 us  [kernel_step(): make_kernel(n_dp, n_zero, mats, rows, dim)(grad_parts, momentum)]
    reduce_scatter x1 -> x0, waiting for transfers between devices: 45.5 us -> none  [on_device(): lax.psum_scatter(contrib.astype(jnp.bfloat16), 'zero', scatter_dimension=...]
    all_gather x1 -> x0, waiting for transfers between devices: 34.7 us -> none  [on_device(): gathered = lax.all_gather(start_rows, 'zero', axis=1, tiled=True)]
    dot_general x5 -> x0, matrix products: 25 us -> none  [the longest x2 12.3 us: orthogonalize(): jnp.dot(poly_term, current, preferred_element_type=jnp.float32)]
    psum x1 -> x0, blocking collectives: 6.29 us -> none  [on_device(): squares = lax.psum(partial_value, 'zero')]
    convert_element_type x4 -> x1, other arithmetic: 7.38 us -> 1.6 us  [kernel_step(): return (nm.astype(jnp.float32), update_rows, copy)]
    unnamed x4 -> x8, local copies, waits for them, and re-layouts: 0.01 us -> 4.04 us
  transfers between devices with their start and end apart: 3 -> 0, of which waited for: 3 -> 0; matrix products, arithmetic and copies ran while one was open for 0% -> 0% of each run, Pallas kernels for 0% -> 0%
where the time goes in v1:
time: 97.2 us; the launch traced here: 96.9 us
  Pallas kernels  82.5 us (85%)
  local copies, waits for them, and re-layouts  6.32 us (7%)
  other arithmetic  5.52 us (6%)
  between operations  2.61 us (3%)
    pallas_call x1, Pallas kernels, kernel_step(): make_kernel(n_dp, n_zero, mats, rows, dim)(grad_parts, momentum)  82.5 us
    unnamed x8, local copies, waits for them, and re-layouts  4.04 us
    dynamic_slice x1, local copies, waits for them, and re-layouts, kernel_step(): update_rows = lax.dynamic_slice_in_dim(update, me * rows, rows, axis=1)  2.29 us

profile of v1, /device:TPU:0, one launch (start us, length us, event | category | flops | bytes accessed | tf_op | source)
XLA Modules:
  0.0 96.9 jit_solution(1732315203057483210)
XLA Ops:
  0.6 1.3 %compare_reduce_fusion = (pred[]{:T(512)}, s32[]{:T(128)}) fusion(s32[3]{0:T(128)} %param.5, s32[]{:T(128)S(6)} %axis_index.12), kind=kLoop, calls=%fused_computation.1 | loop fusion | flops 17 | bytes 21 | tf_op jit(solution)/shard_map/solution.<locals>.kernel_step/reduce | solution.py:334
  3.9 0.0 copy-start.1
  3.9 1.6 %copy-done.1 = f32[3,176,1024]{2,1,0:T(8,128)S(1)} copy-done((f32[3,176,1024]{2,1,0:T(8,128)S(1)}, f32[3,176,1024]{2,1,0:T(8,128)}, u32[]{:S(2)}) %copy-start.1) | copy-done | bytes 2162712
  5.5 0.0 copy-start.2
  5.5 1.2 %copy-done.2 = bf16[1,3,176,1024]{3,2,1,0:T(8,128)(2,1)S(1)} copy-done((bf16[1,3,176,1024]{3,2,1,0:T(8,128)(2,1)S(1)}, bf16[1,3,176,1024]{3,2,1,0:T(8,128)(2,1)}, u32[]{:S(2)}) %copy-start.2) | copy-done | bytes 1081368
  6.7 0.0 copy-start.3
  6.7 82.5 %shard_map.58 = (bf16[3,176,1024]{2,1,0:T(8,128)(2,1)S(1)}, bf16[3,704,1024]{2,1,0:T(8,128)(2,1)S(1)}) custom-call(bf16[1,3,176,1024]{3,2,1,0:T(8,128)(2,1)S(1)} %copy-done.2, f32[3,176,1024]{2,1,0:T(8,128)S(1)} %copy-done.1), custom_call_target="tpu_custom_call" | custom-call | flops 16367222784 | bytes 8650752 | tf_op jit(solution)/shard_map/pallas_call | solution.py:332
  89.2 0.0 copy-start
  89.2 0.0 copy-done.3
  89.2 0.8 compare_reduce_fusion.1
  90.0 1.2 %copy-done = bf16[3,704,1024]{2,1,0:T(8,128)(2,1)} copy-done((bf16[3,704,1024]{2,1,0:T(8,128)(2,1)}, bf16[3,704,1024]{2,1,0:T(8,128)(2,1)S(1)}, u32[]{:S(2)}) %copy-start) | copy-done | bytes 4325400
  91.2 1.8 %dynamic-slice_select_fusion = bf16[1,704,1024]{2,1,0:T(8,128)(2,1)} fusion(bf16[3,704,1024]{2,1,0:T(8,128)(2,1)S(1)} %get-tuple-element.7, s32[]{:T(128)S(6)} %select_n.21, pred[]{:T(512)} %compare_reduce_fusion.1), kind=kLoop, calls=%fused_computation | loop fusion | flops 720896 | bytes 2883589 | tf_op jit(solution)/shard_map/jit(_where)/select_n | solution.py:336
  93.0 2.3 %constant_dynamic-slice_fusion = bf16[3,176,1024]{2,1,0:T(8,128)(2,1)} fusion(bf16[3,704,1024]{2,1,0:T(8,128)(2,1)} %copy-done, s32[]{:T(128)S(6)} %select_n.19), kind=kLoop, calls=%fused_computation.3 | loop fusion | bytes 2162692 | tf_op jit(solution)/shard_map/dynamic_slice | solution.py:337
  95.3 1.6 %convert_element_type.3 = f32[3,176,1024]{2,1,0:T(8,128)} convert(bf16[3,176,1024]{2,1,0:T(8,128)(2,1)S(1)} %get-tuple-element.6) | non-fusion elementwise | flops 540672 | bytes 3244032 | tf_op jit(solution)/shard_map/convert_element_type | solution.py:338
Async XLA Ops:
  3.9 1.6 %copy-start.1 = (f32[3,176,1024]{2,1,0:T(8,128)S(1)}, f32[3,176,1024]{2,1,0:T(8,128)}, u32[]{:S(2)}) copy-start(f32[3,176,1024]{2,1,0:T(8,128)} %momentum.1) | copy-start | bytes 6488068
  5.5 1.2 %copy-start.2 = (bf16[1,3,176,1024]{3,2,1,0:T(8,128)(2,1)S(1)}, bf16[1,3,176,1024]{3,2,1,0:T(8,128)(2,1)}, u32[]{:S(2)}) copy-start(bf16[1,3,176,1024]{3,2,1,0:T(8,128)(2,1)} %grad.1) | copy-start | bytes 3244036
  6.7 82.5 %copy-start.3 = (s32[3]{0:T(128)S(1)}, s32[3]{0:T(128)}, u32[]{:S(2)}) copy-start(s32[3]{0:T(128)} %param.5) | copy-start | bytes 40
  89.2 2.0 %copy-start = (bf16[3,704,1024]{2,1,0:T(8,128)(2,1)}, bf16[3,704,1024]{2,1,0:T(8,128)(2,1)S(1)}, u32[]{:S(2)}) copy-start(bf16[3,704,1024]{2,1,0:T(8,128)(2,1)S(1)} %get-tuple-element.7) | copy-start | bytes 12976132

commit v2 on v1

--- a/solution.py
+++ b/solution.py
@@ -64,14 +64,15 @@
 
 def make_kernel(n_dp, n_zero, mats, rows, dim):
     hid = rows * n_zero
+    half = hid // 2
     n_line = n_dp // 2
     width = dim // n_dp
     out_scale = 0.2 * math.sqrt(dim)
 
     def kernel(
         grad, momentum, nm_out, up_out,
-        x, parts, mom, gram, poly, scale,
-        rs_s, rs_r, s1_s, s1_r, s2_s, s2_r, s3_s, s3_r, s4_s, s4_r, local,
+        x, later, gram, parts, mom, poly, scale,
+        rs_s, rs_r, s1_s, s1_r, s2_s, s2_r, s3_s, s3_r, s4_s, s4_r, gx_s, gx_r, xx_s, xx_r, local,
     ):
         d = lax.axis_index("dp")
         o = lax.axis_index("zero")
@@ -145,7 +146,7 @@
             return pltpu.make_async_copy(x.at[j, row(o), :], nm_out.at[j], local.at[mats + 1 + j])
 
         def up_copy(j):
-            return pltpu.make_async_copy(x.at[j], up_out.at[j], local.at[2 * mats + 1 + j])
+            return pltpu.make_async_copy(later.at[ITERS - 1, j], up_out.at[j], local.at[2 * mats + 1 + j])
 
         peers = [((d + r) % n_dp, o) for r in range(1, n_dp)] + [(d, y_peer), (d, c_peer)]
         barrier = pltpu.get_barrier_semaphore()
@@ -196,6 +197,109 @@
         def phase_e(j):
             for h in range(2):
                 s4_in(j, h).wait_recv()
+
+        def half_rows(c):
+            return pl.ds(pl.multiple_of(c * half, 16), half)
+
+        def gx(j, it, c=None):
+            g = gram.at[j, it, half_rows(ci if c is None else c), :]
+            return remote(g, g, gx_s.at[j, it], gx_r.at[j, it], (d, c_peer))
+
+        def xx(j, it, c=None):
+            v = later.at[it, j, half_rows(ci if c is None else c), :]
+            return remote(v, v, xx_s.at[j, it], xx_r.at[j, it], (d, c_peer))
+
+        mine = half_rows(ci)
+
+        def source(j, it):
+            return x.at[j] if it == 0 else later.at[it - 1, j]
+
+        def gram_op(j, it):
+            src = source(j, it)
+            if it == 0:
+
+                def add(i, acc):
+                    v = src[pl.ds(pl.multiple_of(i * 16, 16), 16), :].astype(jnp.float32)
+                    return acc + v * v
+
+                acc = lax.fori_loop(0, hid // 16, add, jnp.zeros((16, dim), jnp.float32))
+                total = jnp.sum(jnp.sum(acc, axis=0, keepdims=True), axis=1, keepdims=True)
+                scale[j] = jnp.broadcast_to(1.0 / (jnp.sqrt(total) + NORM_EPSILON), scale.shape[1:])
+            else:
+                xx(j, it - 1, 1 - ci).wait_recv()
+            for at, size in column_tiles(hid):
+                g = lax.dot_general(
+                    src[mine, :], src[at : at + size, :], (((1,), (1,)), ((), ())),
+                    preferred_element_type=jnp.float32,
+                )
+                if it == 0:
+                    s = scale[j, 0:1, 0:1]
+                    g = g * s * s
+                gram[j, it, mine, at : at + size] = g.astype(jnp.bfloat16)
+            gx(j, it).start()
+
+        def apply_op(j, it):
+            src = source(j, it)
+            gx(j, it, 1 - ci).wait_recv()
+            for at, size in column_tiles(hid):
+                q = jnp.dot(
+                    gram[j, it, mine, :], gram[j, it, :, at : at + size],
+                    preferred_element_type=jnp.float32,
+                )
+                block = gram[j, it, mine, at : at + size].astype(jnp.float32)
+                poly[:, at : at + size] = (COEF_B * block + COEF_C * q).astype(jnp.bfloat16)
+
+            def apply(i, carry):
+                cols = pl.ds(pl.multiple_of(i * 256, 256), 256)
+                y = COEF_A * src[mine, cols].astype(jnp.float32) + jnp.dot(
+                    poly[...], src[:, cols], preferred_element_type=jnp.float32
+                )
+                if it == 0:
+                    y = y * scale[j, 0:1, 0:1]
+                if it == ITERS - 1:
+                    y = y * out_scale
+                later[it, j, mine, cols] = y.astype(jnp.bfloat16)
+                return carry
+
+            lax.fori_loop(0, dim // 256, apply, 0)
+            xx(j, it).start()
+
+        def finish(j):
+            xx(j, ITERS - 1, 1 - ci).wait_recv()
+            up_copy(j).start()
+
+        phase_a(0)
+        phase_b(0)
+        phase_c(0)
+        phase_a(1)
+        phase_d(0)
+        phase_b(1)
+        phase_c(1)
+        phase_e(0)
+        gram_op(0, 0)
+        phase_a(2)
+        phase_b(2)
+        apply_op(0, 0)
+        gram_op(0, 1)
+        phase_c(2)
+        phase_d(1)
+        phase_e(1)
+        gram_op(1, 0)
+        apply_op(0, 1)
+        apply_op(1, 0)
+        phase_d(2)
+        phase_e(2)
+        gram_op(2, 0)
+        gram_op(1, 1)
+        finish(0)
+        apply_op(2, 0)
+        apply_op(1, 1)
+        gram_op(2, 1)
+        finish(1)
+        apply_op(2, 1)
+        finish(2)
+
+        for j in range(mats):
             for r in range(1, n_dp):
                 rs(j, r).wait_send()
             for r in range(1, n_line):
@@ -206,94 +310,14 @@
                     s3(j, r, h).wait_send()
             for h in range(2):
                 s4(j, h).wait_send()
+            for it in range(ITERS):
+                gx(j, it).wait_send()
+                xx(j, it).wait_send()
             nm_copy(j).wait()
-
-        def ns_step(t):
-            j, it = t // ITERS, t % ITERS
-
-            @pl.when(it == 0)
-            def _():
-                def add(i, acc):
-                    v = x[j, pl.ds(pl.multiple_of(i * 16, 16), 16), :].astype(jnp.float32)
-                    return acc + v * v
-
-                acc = lax.fori_loop(0, hid // 16, add, jnp.zeros((16, dim), jnp.float32))
-                total = jnp.sum(jnp.sum(acc, axis=0, keepdims=True), axis=1, keepdims=True)
-                scale[...] = jnp.broadcast_to(1.0 / (jnp.sqrt(total) + NORM_EPSILON), scale.shape)
-
-            @pl.when(it != 0)
-            def _():
-                scale[...] = jnp.ones(scale.shape, jnp.float32)
-
-            s = scale[0:1, 0:1]
-            for at, size in column_tiles(hid):
-                g = lax.dot_general(
-                    x[j], x[j, at : at + size, :], (((1,), (1,)), ((), ())),
-                    preferred_element_type=jnp.float32,
-                )
-                gram[:, at : at + size] = (g * s * s).astype(jnp.bfloat16)
-            for at, size in column_tiles(hid):
-                block = gram[:, at : at + size]
-                q = jnp.dot(gram[...], block, preferred_element_type=jnp.float32)
-                poly[:, at : at + size] = (COEF_B * block.astype(jnp.float32) + COEF_C * q).astype(
-                    jnp.bfloat16
-                )
-            last = (it == ITERS - 1).astype(jnp.float32)
-            post = s * (1.0 + last * (out_scale - 1.0))
-
-            def apply(i, carry):
-                cols = pl.ds(pl.multiple_of(i * 256, 256), 256)
-                block = x[j, :, cols]
-                y = COEF_A * block.astype(jnp.float32) + jnp.dot(
-                    poly[...], block, preferred_element_type=jnp.float32
-                )
-                x[j, :, cols] = (y * post).astype(jnp.bfloat16)
-                return carry
-
-            lax.fori_loop(0, dim // 256, apply, 0)
-
-        phase_a(0)
-        phase_b(0)
-        phase_c(0)
-        phase_a(1)
-        phase_d(0)
-        phase_b(1)
-        phase_c(1)
-        phase_e(0)
-
-        def step(t, carry):
-            ns_step(t)
-
-            @pl.when(t == 0)
-            def _():
-                phase_a(2)
-                phase_b(2)
-
-            @pl.when(t == 1)
-            def _():
-                up_copy(0).start()
-                phase_c(2)
-                phase_d(1)
-                phase_e(1)
-
-            @pl.when(t == 2)
-            def _():
-                phase_d(2)
-
-            @pl.when(t == 3)
-            def _():
-                up_copy(1).start()
-                phase_e(2)
-
-            return carry
-
-        lax.fori_loop(0, mats * ITERS, step, 0)
-        up_copy(2).start()
-        for j in range(mats):
             up_copy(j).wait()
 
     dma = pltpu.SemaphoreType.DMA
-    flops = mats * ITERS * 2 * hid * hid * (2 * dim + hid)
+    flops = mats * ITERS * hid * hid * (2 * dim + hid)
     return pl.pallas_call(
         kernel,
         out_shape=(
@@ -304,38 +328,92 @@
         out_specs=(pl.BlockSpec(memory_space=pl.ANY),) * 2,
         scratch_shapes=[
             pltpu.VMEM((mats, hid, dim), jnp.bfloat16),
+            pltpu.VMEM((ITERS, mats, hid, dim), jnp.bfloat16),
+            pltpu.VMEM((mats, ITERS, hid, hid), jnp.bfloat16),
             pltpu.VMEM((mats, n_dp, rows, width), jnp.bfloat16),
             pltpu.VMEM((mats, rows, width), jnp.float32),
-            pltpu.VMEM((hid, hid), jnp.bfloat16),
-            pltpu.VMEM((hid, hid), jnp.bfloat16),
-            pltpu.VMEM((8, LANES), jnp.float32),
+            pltpu.VMEM((half, hid), jnp.bfloat16),
+            pltpu.VMEM((mats, 8, LANES), jnp.float32),
             dma((mats, n_dp)), dma((mats, n_dp)),
             dma((mats, n_line)), dma((mats, n_line)),
             dma((mats, n_line)), dma((mats, n_line)),
             dma((mats, n_line, 2)), dma((mats, n_line, 2)),
             dma((mats, 2)), dma((mats, 2)),
+            dma((mats, ITERS)), dma((mats, ITERS)),
+            dma((mats, ITERS)), dma((mats, ITERS)),
             dma((3 * mats + 1,)),
         ],
         cost_estimate=pl.CostEstimate(flops=flops, bytes_accessed=16 * mats * rows * dim, transcendentals=0),
         compiler_params=pltpu.CompilerParams(
-            collective_id=0, has_side_effects=True, vmem_limit_bytes=40 * 1024 * 1024
+            collective_id=0, has_side_effects=True, vmem_limit_bytes=58 * 1024 * 1024
         ),
     )
 
 
+def make_finish(n_zero, mats, rows, dim):
+    hid = rows * n_zero
+
+    def kernel(table, nm, update, nm_out, up_out, own_out, nm_in, nm_wide, zeros, sems):
+        me = lax.axis_index("zero")
+        mine = update.at[:, pl.ds(pl.multiple_of(me * rows, 16), rows), :]
+        nm_load = pltpu.make_async_copy(nm, nm_in, sems.at[2])
+        nm_load.start()
+        up_store = pltpu.make_async_copy(mine, up_out, sems.at[0])
+        up_store.start()
+        count = jnp.int32(0)
+        for j in range(mats):
+            owned = table[j] == me
+            count = count + owned.astype(jnp.int32)
+
+            @pl.when(owned)
+            def _():
+                pltpu.make_async_copy(update.at[j], own_out.at[0], sems.at[1]).start()
+
+        @pl.when(count == 0)
+        def _():
+            zeros[...] = jnp.zeros(zeros.shape, zeros.dtype)
+            pltpu.make_async_copy(zeros, own_out.at[0], sems.at[1]).start()
+
+        nm_load.wait()
+        for j in range(mats):
+            nm_wide[j] = nm_in[j].astype(jnp.float32)
+            pltpu.make_async_copy(nm_wide.at[j], nm_out.at[j], sems.at[3 + j]).start()
+        up_store.wait()
+        pltpu.make_async_copy(update.at[0], own_out.at[0], sems.at[1]).wait()
+        for j in range(mats):
+            pltpu.make_async_copy(nm_wide.at[j], nm_out.at[j], sems.at[3 + j]).wait()
+
+    return pl.pallas_call(
+        kernel,
+        out_shape=(
+            jax.ShapeDtypeStruct((mats, rows, dim), jnp.float32),
+            jax.ShapeDtypeStruct((mats, rows, dim), jnp.bfloat16),
+            jax.ShapeDtypeStruct((1, hid, dim), jnp.bfloat16),
+        ),
+        in_specs=[
+            pl.BlockSpec(memory_space=pltpu.SMEM),
+            pl.BlockSpec(memory_space=pl.ANY),
+            pl.BlockSpec(memory_space=pl.ANY),
+        ],
+        out_specs=(pl.BlockSpec(memory_space=pl.ANY),) * 3,
+        scratch_shapes=[
+            pltpu.VMEM((mats, rows, dim), jnp.bfloat16),
+            pltpu.VMEM((mats, rows, dim), jnp.float32),
+            pltpu.VMEM((hid, dim), jnp.bfloat16),
+            pltpu.SemaphoreType.DMA((3 + mats,)),
+        ],
+        cost_estimate=pl.CostEstimate(flops=0, bytes_accessed=16 * mats * rows * dim, transcendentals=0),
+        compiler_params=pltpu.CompilerParams(vmem_limit_bytes=58 * 1024 * 1024),
+    )
+
+
 def solution(mesh):
     n_dp, n_zero = mesh.shape["dp"], mesh.shape["zero"]
 
     def kernel_step(grad_parts, momentum, owner_table):
         _, mats, rows, dim = grad_parts.shape
-        me = lax.axis_index("zero")
         nm, update = make_kernel(n_dp, n_zero, mats, rows, dim)(grad_parts, momentum)
-        mine = owner_table == me
-        which = jnp.argmax(mine)
-        copy = lax.dynamic_index_in_dim(update, which, 0, keepdims=True)
-        copy = jnp.where(jnp.any(mine), copy, jnp.zeros_like(copy))
-        update_rows = lax.dynamic_slice_in_dim(update, me * rows, rows, axis=1)
-        return nm.astype(jnp.float32), update_rows, copy
+        return make_finish(n_zero, mats, rows, dim)(owner_table, nm, update)
 
     def on_device(grad_parts, momentum, owner_table):
         _, mats, rows, dim = grad_parts.shape

time: 97.2 us -> 163 us (1.68)
  Pallas kernels: 82.5 us -> 162 us
  local copies, waits for them, and re-layouts: 6.32 us -> 0 us
  other arithmetic: 5.52 us -> 0 us
  between operations: 2.61 us -> 0.64 us
    pallas_call x0 -> x1, Pallas kernels: none -> 78.3 us  [kernel_step(): return make_finish(n_zero, mats, rows, dim)(owner_table, nm, update)]
    unnamed x8 -> x0, local copies, waits for them, and re-layouts: 4.04 us -> none
    dynamic_slice x1 -> x0, local copies, waits for them, and re-layouts: 2.29 us -> none  [kernel_step(): update_rows = lax.dynamic_slice_in_dim(update, me * rows, rows, axis=1)]
    select_n x1 -> x0, other arithmetic: 1.84 us -> none  [kernel_step(): copy = jnp.where(jnp.any(mine), copy, jnp.zeros_like(copy))]
    pallas_call x1, Pallas kernels: 82.5 us -> 84.1 us  [kernel_step(): make_kernel(n_dp, n_zero, mats, rows, dim)(grad_parts, momentum)]
where the time goes in v2:
time: 163 us
  Pallas kernels  162 us (99%)
    pallas_call x1, Pallas kernels, kernel_step(): make_kernel(n_dp, n_zero, mats, rows, dim)(grad_parts, momentum)  84.1 us
    pallas_call x1, Pallas kernels, kernel_step(): return make_finish(n_zero, mats, rows, dim)(owner_table, nm, update)  78.3 us

profile of v2, /device:TPU:0, one launch (start us, length us, event | category | flops | bytes accessed | tf_op | source)
XLA Modules:
  0.0 163.0 jit_solution(3477600717150423151)
XLA Ops:
  0.6 84.1 %shard_map.58 = (bf16[3,176,1024]{2,1,0:T(8,128)(2,1)}, bf16[3,704,1024]{2,1,0:T(8,128)(2,1)}) custom-call(bf16[1,3,176,1024]{3,2,1,0:T(8,128)(2,1)} %grad.1, f32[3,176,1024]{2,1,0:T(8,128)} %momentum.1), custom_call_target="tpu_custom_call" | custom-call | flops 8183611392 | bytes 8650752 | tf_op jit(solution)/shard_map/pallas_call | solution.py:415
  84.7 78.3 %shard_map.59 = (f32[3,176,1024]{2,1,0:T(8,128)}, bf16[3,176,1024]{2,1,0:T(8,128)(2,1)}, bf16[1,704,1024]{2,1,0:T(8,128)(2,1)}) custom-call(s32[3]{0:T(128)} %table.1, bf16[3,176,1024]{2,1,0:T(8,128)(2,1)} %get-tuple-element.5.nm, bf16[3,704,1024]{2,1,0:T(8,128)(2,1)} %get-tuple-element.6.update), custom_call_target="tpu_custom_call" | custom-call | bytes 8650752 | tf_op jit(solution)/shard_map/pallas_call | solution.py:416

commit v3 on v2

--- a/solution.py
+++ b/solution.py
@@ -71,7 +71,7 @@
 
     def kernel(
         grad, momentum, nm_out, up_out,
-        x, later, gram, parts, mom, poly, scale,
+        grads, stage, x, full, later, gram, parts, mom, poly, scale,
         rs_s, rs_r, s1_s, s1_r, s2_s, s2_r, s3_s, s3_r, s4_s, s4_r, gx_s, gx_r, xx_s, xx_r, local,
     ):
         d = lax.axis_index("dp")
@@ -88,7 +88,7 @@
             return pl.ds(pl.multiple_of(k * width, LANES), width)
 
         def chunk(j, s, k):
-            return x.at[j, row(s), col(k)]
+            return x.at[j, k, row(s), :]
 
         def line(r):
             return (zi + n_line - r) % n_line
@@ -101,7 +101,7 @@
 
         def rs(j, r):
             p = (d + r) % n_dp
-            return remote(grad.at[0, j, :, col(p)], parts.at[j, r], rs_s.at[j, r], rs_r.at[j, r], (p, o))
+            return remote(stage.at[j, p], parts.at[j, r - 1], rs_s.at[j, r], rs_r.at[j, r], (p, o))
 
         def s1(j, r):
             c = chunk(j, o, d)
@@ -130,46 +130,50 @@
         def s4(j, h, s=None):
             if s is None:
                 s = o if h == 0 else y_peer
-            c = x.at[j, row(s), :]
+            c = x.at[j, :, row(s), :]
             return remote(c, c, s4_s.at[j, h], s4_r.at[j, h], (d, c_peer))
 
         def s4_in(j, h):
             return s4(j, h, c_peer if h == 0 else (1 - yi) * 2 + 1 - ci)
 
-        def own_part(j):
-            return pltpu.make_async_copy(grad.at[0, j, :, col(d)], parts.at[j, 0], local.at[j])
+        def load_grad(j):
+            return pltpu.make_async_copy(grad.at[0, j], grads.at[j], local.at[j])
 
         def own_momentum():
             return pltpu.make_async_copy(momentum.at[:, :, col(d)], mom, local.at[mats])
 
         def nm_copy(j):
-            return pltpu.make_async_copy(x.at[j, row(o), :], nm_out.at[j], local.at[mats + 1 + j])
+            return pltpu.make_async_copy(full.at[j, row(o), :], nm_out.at[j], local.at[mats + 1 + j])
 
         def up_copy(j):
             return pltpu.make_async_copy(later.at[ITERS - 1, j], up_out.at[j], local.at[2 * mats + 1 + j])
 
         peers = [((d + r) % n_dp, o) for r in range(1, n_dp)] + [(d, y_peer), (d, c_peer)]
         barrier = pltpu.get_barrier_semaphore()
+        for j in range(mats):
+            load_grad(j).start()
         own_momentum().start()
-        for j in range(mats):
-            own_part(j).start()
         for to in peers:
             pl.semaphore_signal(barrier, inc=1, device_id=to, device_id_type=MESH)
+        for j in range(mats):
+            load_grad(j).wait()
+            for k in range(n_dp):
+                stage[j, k] = grads[j, :, k * width : (k + 1) * width]
         pl.semaphore_wait(barrier, len(peers))
-        for j in range(mats):
+
+        def send_parts(j):
             for r in range(1, n_dp):
                 rs(j, r).start()
 
         def phase_a(j):
             if j == 0:
                 own_momentum().wait()
-            own_part(j).wait()
             for r in range(1, n_dp):
                 rs(j, r).wait_recv()
-            total = parts[j, 0].astype(jnp.float32)
-            for r in range(1, n_dp):
+            total = stage[j, d].astype(jnp.float32)
+            for r in range(n_dp - 1):
                 total = total + parts[j, r].astype(jnp.float32)
-            x[j, row(o), col(d)] = (MOMENTUM_DECAY * mom[j] + total).astype(jnp.bfloat16)
+            x[j, d, row(o), :] = (MOMENTUM_DECAY * mom[j] + total).astype(jnp.bfloat16)
             s3(j, 0, 0).start()
             s2(j, 0).start()
             for r in range(1, n_line):
@@ -186,7 +190,6 @@
                 s2_in(j, r).wait_recv()
                 s3(j, r, 1).start()
             s4(j, 0).start()
-            nm_copy(j).start()
 
         def phase_d(j):
             for r in range(n_line):
@@ -212,18 +215,19 @@
         mine = half_rows(ci)
 
         def source(j, it):
-            return x.at[j] if it == 0 else later.at[it - 1, j]
+            return full.at[j] if it == 0 else later.at[it - 1, j]
 
         def gram_op(j, it):
             src = source(j, it)
             if it == 0:
-
-                def add(i, acc):
-                    v = src[pl.ds(pl.multiple_of(i * 16, 16), 16), :].astype(jnp.float32)
-                    return acc + v * v
-
-                acc = lax.fori_loop(0, hid // 16, add, jnp.zeros((16, dim), jnp.float32))
-                total = jnp.sum(jnp.sum(acc, axis=0, keepdims=True), axis=1, keepdims=True)
+                acc = jnp.zeros((1, width), jnp.float32)
+                for k in range(n_dp):
+                    v = x[j, k]
+                    full[j, :, k * width : (k + 1) * width] = v
+                    w = v.astype(jnp.float32)
+                    acc = acc + jnp.sum(w * w, axis=0, keepdims=True)
+                nm_copy(j).start()
+                total = jnp.sum(acc, axis=1, keepdims=True)
                 scale[j] = jnp.broadcast_to(1.0 / (jnp.sqrt(total) + NORM_EPSILON), scale.shape[1:])
             else:
                 xx(j, it - 1, 1 - ci).wait_recv()
@@ -268,8 +272,13 @@
             xx(j, ITERS - 1, 1 - ci).wait_recv()
             up_copy(j).start()
 
+        send_parts(0)
+        for r in range(1, n_dp):
+            rs(0, r).wait_send()
+            rs(1, r).start()
         phase_a(0)
         phase_b(0)
+        send_parts(2)
         phase_c(0)
         phase_a(1)
         phase_d(0)
@@ -300,8 +309,9 @@
         finish(2)
 
         for j in range(mats):
-            for r in range(1, n_dp):
-                rs(j, r).wait_send()
+            if j > 0:
+                for r in range(1, n_dp):
+                    rs(j, r).wait_send()
             for r in range(1, n_line):
                 s1(j, r).wait_send()
             for r in range(n_line):
@@ -327,10 +337,13 @@
         in_specs=[pl.BlockSpec(memory_space=pl.ANY)] * 2,
         out_specs=(pl.BlockSpec(memory_space=pl.ANY),) * 2,
         scratch_shapes=[
+            pltpu.VMEM((mats, rows, dim), jnp.bfloat16),
+            pltpu.VMEM((mats, n_dp, rows, width), jnp.bfloat16),
+            pltpu.VMEM((mats, n_dp, hid, width), jnp.bfloat16),
             pltpu.VMEM((mats, hid, dim), jnp.bfloat16),
             pltpu.VMEM((ITERS, mats, hid, dim), jnp.bfloat16),
             pltpu.VMEM((mats, ITERS, hid, hid), jnp.bfloat16),
-            pltpu.VMEM((mats, n_dp, rows, width), jnp.bfloat16),
+            pltpu.VMEM((mats, n_dp - 1, rows, width), jnp.bfloat16),
             pltpu.VMEM((mats, rows, width), jnp.float32),
             pltpu.VMEM((half, hid), jnp.bfloat16),
             pltpu.VMEM((mats, 8, LANES), jnp.float32),
@@ -353,13 +366,13 @@
 def make_finish(n_zero, mats, rows, dim):
     hid = rows * n_zero
 
-    def kernel(table, nm, update, nm_out, up_out, own_out, nm_in, nm_wide, zeros, sems):
+    def kernel(table, nm, update, nm_out, up_out, own_out, nm_in, nm_wide, up, own, sems):
         me = lax.axis_index("zero")
-        mine = update.at[:, pl.ds(pl.multiple_of(me * rows, 16), rows), :]
-        nm_load = pltpu.make_async_copy(nm, nm_in, sems.at[2])
+        rows_mine = update.at[:, pl.ds(pl.multiple_of(me * rows, 16), rows), :]
+        nm_load = pltpu.make_async_copy(nm, nm_in, sems.at[0])
         nm_load.start()
-        up_store = pltpu.make_async_copy(mine, up_out, sems.at[0])
-        up_store.start()
+        up_load = pltpu.make_async_copy(rows_mine, up, sems.at[1])
+        up_load.start()
         count = jnp.int32(0)
         for j in range(mats):
             owned = table[j] == me
@@ -367,21 +380,32 @@
 
             @pl.when(owned)
             def _():
-                pltpu.make_async_copy(update.at[j], own_out.at[0], sems.at[1]).start()
+                pltpu.make_async_copy(update.at[j], own, sems.at[2]).start()
+
+        nm_load.wait()
+        nm_store = []
+        for j in range(mats):
+            nm_wide[j] = nm_in[j].astype(jnp.float32)
+            nm_store.append(pltpu.make_async_copy(nm_wide.at[j], nm_out.at[j], sems.at[5 + j]))
+            nm_store[j].start()
+        up_load.wait()
+        up_store = pltpu.make_async_copy(up, up_out, sems.at[3])
+        up_store.start()
 
         @pl.when(count == 0)
         def _():
-            zeros[...] = jnp.zeros(zeros.shape, zeros.dtype)
-            pltpu.make_async_copy(zeros, own_out.at[0], sems.at[1]).start()
-
-        nm_load.wait()
-        for j in range(mats):
-            nm_wide[j] = nm_in[j].astype(jnp.float32)
-            pltpu.make_async_copy(nm_wide.at[j], nm_out.at[j], sems.at[3 + j]).start()
+            own[...] = jnp.zeros(own.shape, own.dtype)
+
+        @pl.when(count > 0)
+        def _():
+            pltpu.make_async_copy(update.at[0], own, sems.at[2]).wait()
+
+        own_store = pltpu.make_async_copy(own, own_out.at[0], sems.at[4])
+        own_store.start()
         up_store.wait()
-        pltpu.make_async_copy(update.at[0], own_out.at[0], sems.at[1]).wait()
-        for j in range(mats):
-            pltpu.make_async_copy(nm_wide.at[j], nm_out.at[j], sems.at[3 + j]).wait()
+        own_store.wait()
+        for j in range(mats):
+            nm_store[j].wait()
 
     return pl.pallas_call(
         kernel,
@@ -399,8 +423,9 @@
         scratch_shapes=[
             pltpu.VMEM((mats, rows, dim), jnp.bfloat16),
             pltpu.VMEM((mats, rows, dim), jnp.float32),
+            pltpu.VMEM((mats, rows, dim), jnp.bfloat16),
             pltpu.VMEM((hid, dim), jnp.bfloat16),
-            pltpu.SemaphoreType.DMA((3 + mats,)),
+            pltpu.SemaphoreType.DMA((5 + mats,)),
         ],
         cost_estimate=pl.CostEstimate(flops=0, bytes_accessed=16 * mats * rows * dim, transcendentals=0),
         compiler_params=pltpu.CompilerParams(vmem_limit_bytes=58 * 1024 * 1024),

time: 163 us -> 83.8 us (0.51)
  Pallas kernels: 162 us -> 83 us
    pallas_call x1, Pallas kernels: 78.3 us -> 4.19 us  [kernel_step(): return make_finish(n_zero, mats, rows, dim)(owner_table, nm, update)]
    pallas_call x1, Pallas kernels: 84.1 us -> 78.9 us  [kernel_step(): make_kernel(n_dp, n_zero, mats, rows, dim)(grad_parts, momentum)]
where the time goes in v3:
time: 83.8 us; the launch traced here: 83.7 us
  Pallas kernels  83 us (99%)
    pallas_call x1, Pallas kernels, kernel_step(): make_kernel(n_dp, n_zero, mats, rows, dim)(grad_parts, momentum)  78.9 us
    pallas_call x1, Pallas kernels, kernel_step(): return make_finish(n_zero, mats, rows, dim)(owner_table, nm, update)  4.19 us

profile of v3, /device:TPU:0, one launch (start us, length us, event | category | flops | bytes accessed | tf_op | source)
XLA Modules:
  0.0 83.7 jit_solution(17900028633170754684)
XLA Ops:
  0.6 78.9 %shard_map.58 = (bf16[3,176,1024]{2,1,0:T(8,128)(2,1)}, bf16[3,704,1024]{2,1,0:T(8,128)(2,1)}) custom-call(bf16[1,3,176,1024]{3,2,1,0:T(8,128)(2,1)} %grad.1, f32[3,176,1024]{2,1,0:T(8,128)} %momentum.1), custom_call_target="tpu_custom_call" | custom-call | flops 8183611392 | bytes 8650752 | tf_op jit(solution)/shard_map/pallas_call | solution.py:440
  79.5 4.2 %shard_map.59 = (f32[3,176,1024]{2,1,0:T(8,128)}, bf16[3,176,1024]{2,1,0:T(8,128)(2,1)}, bf16[1,704,1024]{2,1,0:T(8,128)(2,1)}) custom-call(s32[3]{0:T(128)} %table.1, bf16[3,176,1024]{2,1,0:T(8,128)(2,1)} %get-tuple-element.5.nm, bf16[3,704,1024]{2,1,0:T(8,128)(2,1)} %get-tuple-element.6.update), custom_call_target="tpu_custom_call" | custom-call | bytes 8650752 | tf_op jit(solution)/shard_map/pallas_call | solution.py:441

commit v4 on v3

--- a/solution.py
+++ b/solution.py
@@ -71,8 +71,8 @@
 
     def kernel(
         grad, momentum, nm_out, up_out,
-        grads, stage, x, full, later, gram, parts, mom, poly, scale,
-        rs_s, rs_r, s1_s, s1_r, s2_s, s2_r, s3_s, s3_r, s4_s, s4_r, gx_s, gx_r, xx_s, xx_r, local,
+        grads, stage, pairs_in, pairs, x, full, later, gram, parts, mom, poly, scale,
+        ra_s, ra_r, rs_s, rs_r, s1_s, s1_r, s2_s, s2_r, s3_s, s3_r, s4_s, s4_r, gx_s, gx_r, xx_s, xx_r, local,
     ):
         d = lax.axis_index("dp")
         o = lax.axis_index("zero")
@@ -99,9 +99,13 @@
                 device_id=to, device_id_type=MESH,
             )
 
-        def rs(j, r):
-            p = (d + r) % n_dp
-            return remote(stage.at[j, p], parts.at[j, r - 1], rs_s.at[j, r], rs_r.at[j, r], (p, o))
+        def ra(j, r):
+            k = ((zi + r) % n_line) * 2 + 1 - xi
+            return remote(stage.at[j, k], pairs_in.at[j, r], ra_s.at[j, r], ra_r.at[j, r], (x_peer, o))
+
+        def rb(j, r):
+            to = (((zi + r) % n_line) * 2 + xi, o)
+            return remote(pairs.at[j, r - 1], parts.at[j, r - 1], rs_s.at[j, r], rs_r.at[j, r], to)
 
         def s1(j, r):
             c = chunk(j, o, d)
@@ -148,7 +152,8 @@
         def up_copy(j):
             return pltpu.make_async_copy(later.at[ITERS - 1, j], up_out.at[j], local.at[2 * mats + 1 + j])
 
-        peers = [((d + r) % n_dp, o) for r in range(1, n_dp)] + [(d, y_peer), (d, c_peer)]
+        peers = [(((zi + r) % n_line) * 2 + xi, o) for r in range(1, n_line)]
+        peers += [(x_peer, o), (d, y_peer), (d, c_peer)]
         barrier = pltpu.get_barrier_semaphore()
         for j in range(mats):
             load_grad(j).start()
@@ -162,16 +167,27 @@
         pl.semaphore_wait(barrier, len(peers))
 
         def send_parts(j):
-            for r in range(1, n_dp):
-                rs(j, r).start()
+            for r in [*range(1, n_line), 0]:
+                ra(j, r).start()
+
+        def pair(j, r):
+            k = ((zi + r) % n_line) * 2 + xi
+            return stage[j, k].astype(jnp.float32) + pairs_in[j, r].astype(jnp.float32)
+
+        def phase_p(j):
+            for r in range(1, n_line):
+                ra(j, r).wait_recv()
+                pairs[j, r - 1] = pair(j, r).astype(jnp.bfloat16)
+                rb(j, r).start()
 
         def phase_a(j):
             if j == 0:
                 own_momentum().wait()
-            for r in range(1, n_dp):
-                rs(j, r).wait_recv()
-            total = stage[j, d].astype(jnp.float32)
-            for r in range(n_dp - 1):
+            ra(j, 0).wait_recv()
+            for r in range(1, n_line):
+                rb(j, r).wait_recv()
+            total = pair(j, 0)
+            for r in range(n_line - 1):
                 total = total + parts[j, r].astype(jnp.float32)
             x[j, d, row(o), :] = (MOMENTUM_DECAY * mom[j] + total).astype(jnp.bfloat16)
             s3(j, 0, 0).start()
@@ -273,12 +289,13 @@
             up_copy(j).start()
 
         send_parts(0)
-        for r in range(1, n_dp):
-            rs(0, r).wait_send()
-            rs(1, r).start()
+        send_parts(1)
+        phase_p(0)
+        send_parts(2)
+        phase_p(1)
         phase_a(0)
         phase_b(0)
-        send_parts(2)
+        phase_p(2)
         phase_c(0)
         phase_a(1)
         phase_d(0)
@@ -309,10 +326,10 @@
         finish(2)
 
         for j in range(mats):
-            if j > 0:
-                for r in range(1, n_dp):
-                    rs(j, r).wait_send()
+            for r in range(n_line):
+                ra(j, r).wait_send()
             for r in range(1, n_line):
+                rb(j, r).wait_send()
                 s1(j, r).wait_send()
             for r in range(n_line):
                 s2(j, r).wait_send()
@@ -339,15 +356,18 @@
         scratch_shapes=[
             pltpu.VMEM((mats, rows, dim), jnp.bfloat16),
             pltpu.VMEM((mats, n_dp, rows, width), jnp.bfloat16),
+            pltpu.VMEM((mats, n_line, rows, width), jnp.bfloat16),
+            pltpu.VMEM((mats, n_line - 1, rows, width), jnp.bfloat16),
             pltpu.VMEM((mats, n_dp, hid, width), jnp.bfloat16),
             pltpu.VMEM((mats, hid, dim), jnp.bfloat16),
             pltpu.VMEM((ITERS, mats, hid, dim), jnp.bfloat16),
             pltpu.VMEM((mats, ITERS, hid, hid), jnp.bfloat16),
-            pltpu.VMEM((mats, n_dp - 1, rows, width), jnp.bfloat16),
+            pltpu.VMEM((mats, n_line - 1, rows, width), jnp.bfloat16),
             pltpu.VMEM((mats, rows, width), jnp.float32),
             pltpu.VMEM((half, hid), jnp.bfloat16),
             pltpu.VMEM((mats, 8, LANES), jnp.float32),
-            dma((mats, n_dp)), dma((mats, n_dp)),
+            dma((mats, n_line)), dma((mats, n_line)),
+            dma((mats, n_line)), dma((mats, n_line)),
             dma((mats, n_line)), dma((mats, n_line)),
             dma((mats, n_line)), dma((mats, n_line)),
             dma((mats, n_line, 2)), dma((mats, n_line, 2)),

time: 83.8 us -> 75.4 us (0.90)
  Pallas kernels: 83 us -> 74.6 us
    pallas_call x1, Pallas kernels: 78.9 us -> 70.5 us  [kernel_step(): make_kernel(n_dp, n_zero, mats, rows, dim)(grad_parts, momentum)]
where the time goes in v4:
time: 75.4 us; the launch traced here: 75.3 us
  Pallas kernels  74.6 us (99%)
    pallas_call x1, Pallas kernels, kernel_step(): make_kernel(n_dp, n_zero, mats, rows, dim)(grad_parts, momentum)  70.5 us
    pallas_call x1, Pallas kernels, kernel_step(): return make_finish(n_zero, mats, rows, dim)(owner_table, nm, update)  4.19 us

profile of v4, /device:TPU:0, one launch (start us, length us, event | category | flops | bytes accessed | tf_op | source)
XLA Modules:
  0.0 75.3 jit_solution(5260950962099645967)
XLA Ops:
  0.6 70.5 %shard_map.58 = (bf16[3,176,1024]{2,1,0:T(8,128)(2,1)}, bf16[3,704,1024]{2,1,0:T(8,128)(2,1)}) custom-call(bf16[1,3,176,1024]{3,2,1,0:T(8,128)(2,1)} %grad.1, f32[3,176,1024]{2,1,0:T(8,128)} %momentum.1), custom_call_target="tpu_custom_call" | custom-call | flops 8183611392 | bytes 8650752 | tf_op jit(solution)/shard_map/pallas_call | solution.py:460
  71.1 4.2 %shard_map.59 = (f32[3,176,1024]{2,1,0:T(8,128)}, bf16[3,176,1024]{2,1,0:T(8,128)(2,1)}, bf16[1,704,1024]{2,1,0:T(8,128)(2,1)}) custom-call(s32[3]{0:T(128)} %table.1, bf16[3,176,1024]{2,1,0:T(8,128)(2,1)} %get-tuple-element.5.nm, bf16[3,704,1024]{2,1,0:T(8,128)(2,1)} %get-tuple-element.6.update), custom_call_target="tpu_custom_call" | custom-call | bytes 8650752 | tf_op jit(solution)/shard_map/pallas_call | solution.py:461

commit v5 on v4

--- a/solution.py
+++ b/solution.py
@@ -65,6 +65,7 @@
 def make_kernel(n_dp, n_zero, mats, rows, dim):
     hid = rows * n_zero
     half = hid // 2
+    gram_tiles = len(column_tiles(hid))
     n_line = n_dp // 2
     width = dim // n_dp
     out_scale = 0.2 * math.sqrt(dim)
@@ -160,11 +161,11 @@
         own_momentum().start()
         for to in peers:
             pl.semaphore_signal(barrier, inc=1, device_id=to, device_id_type=MESH)
-        for j in range(mats):
+
+        def put_together(j):
             load_grad(j).wait()
             for k in range(n_dp):
                 stage[j, k] = grads[j, :, k * width : (k + 1) * width]
-        pl.semaphore_wait(barrier, len(peers))
 
         def send_parts(j):
             for r in [*range(1, n_line), 0]:
@@ -220,13 +221,23 @@
         def half_rows(c):
             return pl.ds(pl.multiple_of(c * half, 16), half)
 
-        def gx(j, it, c=None):
-            g = gram.at[j, it, half_rows(ci if c is None else c), :]
-            return remote(g, g, gx_s.at[j, it], gx_r.at[j, it], (d, c_peer))
-
-        def xx(j, it, c=None):
-            v = later.at[it, j, half_rows(ci if c is None else c), :]
-            return remote(v, v, xx_s.at[j, it], xx_r.at[j, it], (d, c_peer))
+        def gx(j, it, n, c=None):
+            at, size = column_tiles(hid)[n]
+            g = gram.at[j, it, half_rows(ci if c is None else c), at : at + size]
+            return remote(g, g, gx_s.at[j, it, n], gx_r.at[j, it, n], (d, c_peer))
+
+        def xx(j, it, n, c=None):
+            cols = pl.ds(pl.multiple_of(n * 256, 256), 256)
+            v = later.at[it, j, half_rows(ci if c is None else c), cols]
+            return remote(v, v, xx_s.at[j, it, n], xx_r.at[j, it, n], (d, c_peer))
+
+        def gx_wait(j, it):
+            for n in range(gram_tiles):
+                gx(j, it, n, 1 - ci).wait_recv()
+
+        def xx_wait(j, it):
+            for n in range(dim // 256):
+                xx(j, it, n, 1 - ci).wait_recv()
 
         mine = half_rows(ci)
 
@@ -246,8 +257,8 @@
                 total = jnp.sum(acc, axis=1, keepdims=True)
                 scale[j] = jnp.broadcast_to(1.0 / (jnp.sqrt(total) + NORM_EPSILON), scale.shape[1:])
             else:
-                xx(j, it - 1, 1 - ci).wait_recv()
-            for at, size in column_tiles(hid):
+                xx_wait(j, it - 1)
+            for n, (at, size) in enumerate(column_tiles(hid)):
                 g = lax.dot_general(
                     src[mine, :], src[at : at + size, :], (((1,), (1,)), ((), ())),
                     preferred_element_type=jnp.float32,
@@ -256,11 +267,11 @@
                     s = scale[j, 0:1, 0:1]
                     g = g * s * s
                 gram[j, it, mine, at : at + size] = g.astype(jnp.bfloat16)
-            gx(j, it).start()
+                gx(j, it, n).start()
 
         def apply_op(j, it):
             src = source(j, it)
-            gx(j, it, 1 - ci).wait_recv()
+            gx_wait(j, it)
             for at, size in column_tiles(hid):
                 q = jnp.dot(
                     gram[j, it, mine, :], gram[j, it, :, at : at + size],
@@ -279,46 +290,49 @@
                 if it == ITERS - 1:
                     y = y * out_scale
                 later[it, j, mine, cols] = y.astype(jnp.bfloat16)
+                xx(j, it, i).start()
                 return carry
 
             lax.fori_loop(0, dim // 256, apply, 0)
-            xx(j, it).start()
 
         def finish(j):
-            xx(j, ITERS - 1, 1 - ci).wait_recv()
+            xx_wait(j, ITERS - 1)
             up_copy(j).start()
 
-        send_parts(0)
-        send_parts(1)
+        put_together(0)
+        pl.semaphore_wait(barrier, len(peers))
+        for j in range(mats):
+            if j > 0:
+                put_together(j)
+            send_parts(j)
         phase_p(0)
-        send_parts(2)
         phase_p(1)
         phase_a(0)
+        phase_p(2)
+        phase_a(1)
         phase_b(0)
-        phase_p(2)
         phase_c(0)
-        phase_a(1)
+        phase_a(2)
+        phase_b(1)
         phase_d(0)
-        phase_b(1)
         phase_c(1)
+        phase_b(2)
         phase_e(0)
         gram_op(0, 0)
-        phase_a(2)
-        phase_b(2)
-        apply_op(0, 0)
-        gram_op(0, 1)
         phase_c(2)
         phase_d(1)
+        apply_op(0, 0)
         phase_e(1)
         gram_op(1, 0)
-        apply_op(0, 1)
+        phase_d(2)
+        gram_op(0, 1)
         apply_op(1, 0)
-        phase_d(2)
         phase_e(2)
         gram_op(2, 0)
+        apply_op(0, 1)
         gram_op(1, 1)
+        apply_op(2, 0)
         finish(0)
-        apply_op(2, 0)
         apply_op(1, 1)
         gram_op(2, 1)
         finish(1)
@@ -338,8 +352,10 @@
             for h in range(2):
                 s4(j, h).wait_send()
             for it in range(ITERS):
-                gx(j, it).wait_send()
-                xx(j, it).wait_send()
+                for n in range(gram_tiles):
+                    gx(j, it, n).wait_send()
+                for n in range(dim // 256):
+                    xx(j, it, n).wait_send()
             nm_copy(j).wait()
             up_copy(j).wait()
 
@@ -372,8 +388,8 @@
             dma((mats, n_line)), dma((mats, n_line)),
             dma((mats, n_line, 2)), dma((mats, n_line, 2)),
             dma((mats, 2)), dma((mats, 2)),
-            dma((mats, ITERS)), dma((mats, ITERS)),
-            dma((mats, ITERS)), dma((mats, ITERS)),
+            dma((mats, ITERS, gram_tiles)), dma((mats, ITERS, gram_tiles)),
+            dma((mats, ITERS, dim // 256)), dma((mats, ITERS, dim // 256)),
             dma((3 * mats + 1,)),
         ],
         cost_estimate=pl.CostEstimate(flops=flops, bytes_accessed=16 * mats * rows * dim, transcendentals=0),

time: 75.4 us -> 72.2 us (0.958)
  Pallas kernels: 74.6 us -> 71.2 us
    pallas_call x1, Pallas kernels: 70.5 us -> 67 us  [kernel_step(): make_kernel(n_dp, n_zero, mats, rows, dim)(grad_parts, momentum)]
where the time goes in v5:
time: 72.2 us; the launch traced here: 72 us
  Pallas kernels  71.2 us (99%)
  between operations  0.8 us (1%)
    pallas_call x1, Pallas kernels, kernel_step(): make_kernel(n_dp, n_zero, mats, rows, dim)(grad_parts, momentum)  67 us
    pallas_call x1, Pallas kernels, kernel_step(): return make_finish(n_zero, mats, rows, dim)(owner_table, nm, update)  4.19 us

profile of v5, /device:TPU:0, one launch (start us, length us, event | category | flops | bytes accessed | tf_op | source)
XLA Modules:
  0.0 72.0 jit_solution(13831047365708149913)
XLA Ops:
  0.6 67.0 %shard_map.58 = (bf16[3,176,1024]{2,1,0:T(8,128)(2,1)}, bf16[3,704,1024]{2,1,0:T(8,128)(2,1)}) custom-call(bf16[1,3,176,1024]{3,2,1,0:T(8,128)(2,1)} %grad.1, f32[3,176,1024]{2,1,0:T(8,128)} %momentum.1), custom_call_target="tpu_custom_call" | custom-call | flops 8183611392 | bytes 8650752 | tf_op jit(solution)/shard_map/pallas_call | solution.py:476
  67.7 4.2 %shard_map.59 = (f32[3,176,1024]{2,1,0:T(8,128)}, bf16[3,176,1024]{2,1,0:T(8,128)(2,1)}, bf16[1,704,1024]{2,1,0:T(8,128)(2,1)}) custom-call(s32[3]{0:T(128)} %table.1, bf16[3,176,1024]{2,1,0:T(8,128)(2,1)} %get-tuple-element.5.nm, bf16[3,704,1024]{2,1,0:T(8,128)(2,1)} %get-tuple-element.6.update), custom_call_target="tpu_custom_call" | custom-call | bytes 8650752 | tf_op jit(solution)/shard_map/pallas_call | solution.py:477

commit v6 on v5

--- a/solution.py
+++ b/solution.py
@@ -66,6 +66,7 @@
     hid = rows * n_zero
     half = hid // 2
     gram_tiles = len(column_tiles(hid))
+    wide = 512 if dim % 512 == 0 else 256
     n_line = n_dp // 2
     width = dim // n_dp
     out_scale = 0.2 * math.sqrt(dim)
@@ -227,7 +228,7 @@
             return remote(g, g, gx_s.at[j, it, n], gx_r.at[j, it, n], (d, c_peer))
 
         def xx(j, it, n, c=None):
-            cols = pl.ds(pl.multiple_of(n * 256, 256), 256)
+            cols = slice(n * wide, (n + 1) * wide)
             v = later.at[it, j, half_rows(ci if c is None else c), cols]
             return remote(v, v, xx_s.at[j, it, n], xx_r.at[j, it, n], (d, c_peer))
 
@@ -236,7 +237,7 @@
                 gx(j, it, n, 1 - ci).wait_recv()
 
         def xx_wait(j, it):
-            for n in range(dim // 256):
+            for n in range(dim // wide):
                 xx(j, it, n, 1 - ci).wait_recv()
 
         mine = half_rows(ci)
@@ -258,30 +259,25 @@
                 scale[j] = jnp.broadcast_to(1.0 / (jnp.sqrt(total) + NORM_EPSILON), scale.shape[1:])
             else:
                 xx_wait(j, it - 1)
-            for n, (at, size) in enumerate(column_tiles(hid)):
-                g = lax.dot_general(
-                    src[mine, :], src[at : at + size, :], (((1,), (1,)), ((), ())),
-                    preferred_element_type=jnp.float32,
-                )
-                if it == 0:
-                    s = scale[j, 0:1, 0:1]
-                    g = g * s * s
-                gram[j, it, mine, at : at + size] = g.astype(jnp.bfloat16)
+            g = lax.dot_general(
+                src[mine, :], src[...], (((1,), (1,)), ((), ())),
+                preferred_element_type=jnp.float32,
+            )
+            if it == 0:
+                s = scale[j, 0:1, 0:1]
+                g = g * s * s
+            gram[j, it, mine, :] = g.astype(jnp.bfloat16)
+            for n in range(gram_tiles):
                 gx(j, it, n).start()
 
         def apply_op(j, it):
             src = source(j, it)
             gx_wait(j, it)
-            for at, size in column_tiles(hid):
-                q = jnp.dot(
-                    gram[j, it, mine, :], gram[j, it, :, at : at + size],
-                    preferred_element_type=jnp.float32,
-                )
-                block = gram[j, it, mine, at : at + size].astype(jnp.float32)
-                poly[:, at : at + size] = (COEF_B * block + COEF_C * q).astype(jnp.bfloat16)
-
-            def apply(i, carry):
-                cols = pl.ds(pl.multiple_of(i * 256, 256), 256)
+            q = jnp.dot(gram[j, it, mine, :], gram[j, it], preferred_element_type=jnp.float32)
+            own = gram[j, it, mine, :].astype(jnp.float32)
+            poly[...] = (COEF_B * own + COEF_C * q).astype(jnp.bfloat16)
+            for n in range(dim // wide):
+                cols = slice(n * wide, (n + 1) * wide)
                 y = COEF_A * src[mine, cols].astype(jnp.float32) + jnp.dot(
                     poly[...], src[:, cols], preferred_element_type=jnp.float32
                 )
@@ -290,10 +286,7 @@
                 if it == ITERS - 1:
                     y = y * out_scale
                 later[it, j, mine, cols] = y.astype(jnp.bfloat16)
-                xx(j, it, i).start()
-                return carry
-
-            lax.fori_loop(0, dim // 256, apply, 0)
+                xx(j, it, n).start()
 
         def finish(j):
             xx_wait(j, ITERS - 1)
@@ -354,7 +347,7 @@
             for it in range(ITERS):
                 for n in range(gram_tiles):
                     gx(j, it, n).wait_send()
-                for n in range(dim // 256):
+                for n in range(dim // wide):
                     xx(j, it, n).wait_send()
             nm_copy(j).wait()
             up_copy(j).wait()
@@ -389,7 +382,7 @@
             dma((mats, n_line, 2)), dma((mats, n_line, 2)),
             dma((mats, 2)), dma((mats, 2)),
             dma((mats, ITERS, gram_tiles)), dma((mats, ITERS, gram_tiles)),
-            dma((mats, ITERS, dim // 256)), dma((mats, ITERS, dim // 256)),
+            dma((mats, ITERS, dim // wide)), dma((mats, ITERS, dim // wide)),
             dma((3 * mats + 1,)),
         ],
         cost_estimate=pl.CostEstimate(flops=flops, bytes_accessed=16 * mats * rows * dim, transcendentals=0),
@@ -404,11 +397,22 @@
 
     def kernel(table, nm, update, nm_out, up_out, own_out, nm_in, nm_wide, up, own, sems):
         me = lax.axis_index("zero")
-        rows_mine = update.at[:, pl.ds(pl.multiple_of(me * rows, 16), rows), :]
-        nm_load = pltpu.make_async_copy(nm, nm_in, sems.at[0])
-        nm_load.start()
-        up_load = pltpu.make_async_copy(rows_mine, up, sems.at[1])
-        up_load.start()
+        rows_mine = pl.ds(pl.multiple_of(me * rows, 16), rows)
+        copy = pltpu.make_async_copy
+
+        def part(q):
+            return pl.ds(q * rows, rows)
+
+        def own_load(j, q):
+            return copy(update.at[j, part(q), :], own.at[part(q), :], sems.at[2, q])
+
+        nm_load = [copy(nm.at[j], nm_in.at[j], sems.at[0, j]) for j in range(mats)]
+        up_load = [copy(update.at[j, rows_mine, :], up.at[j], sems.at[1, j]) for j in range(mats)]
+        nm_store = [copy(nm_wide.at[j], nm_out.at[j], sems.at[3, j]) for j in range(mats)]
+        up_store = [copy(up.at[j], up_out.at[j], sems.at[4, j]) for j in range(mats)]
+        own_store = [copy(own.at[part(q), :], own_out.at[0, part(q), :], sems.at[5, q]) for q in range(n_zero)]
+        for load in nm_load + up_load:
+            load.start()
         count = jnp.int32(0)
         for j in range(mats):
             owned = table[j] == me
@@ -416,32 +420,30 @@
 
             @pl.when(owned)
             def _():
-                pltpu.make_async_copy(update.at[j], own, sems.at[2]).start()
-
-        nm_load.wait()
-        nm_store = []
+                for q in range(n_zero):
+                    own_load(j, q).start()
+
         for j in range(mats):
+            nm_load[j].wait()
             nm_wide[j] = nm_in[j].astype(jnp.float32)
-            nm_store.append(pltpu.make_async_copy(nm_wide.at[j], nm_out.at[j], sems.at[5 + j]))
             nm_store[j].start()
-        up_load.wait()
-        up_store = pltpu.make_async_copy(up, up_out, sems.at[3])
-        up_store.start()
+        for j in range(mats):
+            up_load[j].wait()
+            up_store[j].start()
 
         @pl.when(count == 0)
         def _():
             own[...] = jnp.zeros(own.shape, own.dtype)
 
-        @pl.when(count > 0)
-        def _():
-            pltpu.make_async_copy(update.at[0], own, sems.at[2]).wait()
-
-        own_store = pltpu.make_async_copy(own, own_out.at[0], sems.at[4])
-        own_store.start()
-        up_store.wait()
-        own_store.wait()
-        for j in range(mats):
-            nm_store[j].wait()
+        for q in range(n_zero):
+
+            @pl.when(count > 0)
+            def _():
+                own_load(0, q).wait()
+
+            own_store[q].start()
+        for store in nm_store + up_store + own_store:
+            store.wait()
 
     return pl.pallas_call(
         kernel,
@@ -461,7 +463,7 @@
             pltpu.VMEM((mats, rows, dim), jnp.float32),
             pltpu.VMEM((mats, rows, dim), jnp.bfloat16),
             pltpu.VMEM((hid, dim), jnp.bfloat16),
-            pltpu.SemaphoreType.DMA((5 + mats,)),
+            pltpu.SemaphoreType.DMA((6, max(mats, n_zero))),
         ],
         cost_estimate=pl.CostEstimate(flops=0, bytes_accessed=16 * mats * rows * dim, transcendentals=0),
         compiler_params=pltpu.CompilerParams(vmem_limit_bytes=58 * 1024 * 1024),

time: 72.2 us -> 68.2 us (0.945)
  Pallas kernels: 71.2 us -> 67.5 us
    pallas_call x1, Pallas kernels: 67 us -> 62.7 us  [kernel_step(): make_kernel(n_dp, n_zero, mats, rows, dim)(grad_parts, momentum)]
where the time goes in v6:
time: 68.2 us; the launch traced here: 68.1 us
  Pallas kernels  67.5 us (99%)
    pallas_call x1, Pallas kernels, kernel_step(): make_kernel(n_dp, n_zero, mats, rows, dim)(grad_parts, momentum)  62.7 us
    pallas_call x1, Pallas kernels, kernel_step(): return make_finish(n_zero, mats, rows, dim)(owner_table, nm, update)  4.74 us

profile of v6, /device:TPU:0, one launch (start us, length us, event | category | flops | bytes accessed | tf_op | source)
XLA Modules:
  0.0 68.1 jit_solution(8380329965709390538)
XLA Ops:
  0.6 62.7 %shard_map.58 = (bf16[3,176,1024]{2,1,0:T(8,128)(2,1)}, bf16[3,704,1024]{2,1,0:T(8,128)(2,1)}) custom-call(bf16[1,3,176,1024]{3,2,1,0:T(8,128)(2,1)} %grad.1, f32[3,176,1024]{2,1,0:T(8,128)} %momentum.1), custom_call_target="tpu_custom_call" | custom-call | flops 8183611392 | bytes 8650752 | tf_op jit(solution)/shard_map/pallas_call | solution.py:478
  63.4 4.7 %shard_map.59 = (f32[3,176,1024]{2,1,0:T(8,128)}, bf16[3,176,1024]{2,1,0:T(8,128)(2,1)}, bf16[1,704,1024]{2,1,0:T(8,128)(2,1)}) custom-call(s32[3]{0:T(128)} %table.1, bf16[3,176,1024]{2,1,0:T(8,128)(2,1)} %get-tuple-element.5.nm, bf16[3,704,1024]{2,1,0:T(8,128)(2,1)} %get-tuple-element.6.update), custom_call_target="tpu_custom_call" | custom-call | bytes 8650752 | tf_op jit(solution)/shard_map/pallas_call | solution.py:479

commit v7 on v6

--- a/solution.py
+++ b/solution.py
@@ -151,8 +151,10 @@
         def nm_copy(j):
             return pltpu.make_async_copy(full.at[j, row(o), :], nm_out.at[j], local.at[mats + 1 + j])
 
-        def up_copy(j):
-            return pltpu.make_async_copy(later.at[ITERS - 1, j], up_out.at[j], local.at[2 * mats + 1 + j])
+        def up_copy(j, c):
+            part = pl.ds(pl.multiple_of(c * half, 16), half)
+            sem = local.at[2 * mats + 1 + j] if c is ci else local.at[3 * mats + 1 + j]
+            return pltpu.make_async_copy(later.at[ITERS - 1, j, part, :], up_out.at[j, part, :], sem)
 
         peers = [(((zi + r) % n_line) * 2 + xi, o) for r in range(1, n_line)]
         peers += [(x_peer, o), (d, y_peer), (d, c_peer)]
@@ -287,10 +289,12 @@
                     y = y * out_scale
                 later[it, j, mine, cols] = y.astype(jnp.bfloat16)
                 xx(j, it, n).start()
+            if it == ITERS - 1:
+                up_copy(j, ci).start()
 
         def finish(j):
             xx_wait(j, ITERS - 1)
-            up_copy(j).start()
+            up_copy(j, 1 - ci).start()
 
         put_together(0)
         pl.semaphore_wait(barrier, len(peers))
@@ -308,24 +312,24 @@
         phase_a(2)
         phase_b(1)
         phase_d(0)
+        phase_e(0)
+        gram_op(0, 0)
         phase_c(1)
         phase_b(2)
-        phase_e(0)
-        gram_op(0, 0)
+        apply_op(0, 0)
         phase_c(2)
         phase_d(1)
-        apply_op(0, 0)
         phase_e(1)
         gram_op(1, 0)
+        gram_op(0, 1)
         phase_d(2)
-        gram_op(0, 1)
         apply_op(1, 0)
+        apply_op(0, 1)
         phase_e(2)
         gram_op(2, 0)
-        apply_op(0, 1)
         gram_op(1, 1)
+        finish(0)
         apply_op(2, 0)
-        finish(0)
         apply_op(1, 1)
         gram_op(2, 1)
         finish(1)
@@ -350,7 +354,8 @@
                 for n in range(dim // wide):
                     xx(j, it, n).wait_send()
             nm_copy(j).wait()
-            up_copy(j).wait()
+            up_copy(j, ci).wait()
+            up_copy(j, 1 - ci).wait()
 
     dma = pltpu.SemaphoreType.DMA
     flops = mats * ITERS * hid * hid * (2 * dim + hid)
@@ -383,7 +388,7 @@
             dma((mats, 2)), dma((mats, 2)),
             dma((mats, ITERS, gram_tiles)), dma((mats, ITERS, gram_tiles)),
             dma((mats, ITERS, dim // wide)), dma((mats, ITERS, dim // wide)),
-            dma((3 * mats + 1,)),
+            dma((4 * mats + 1,)),
         ],
         cost_estimate=pl.CostEstimate(flops=flops, bytes_accessed=16 * mats * rows * dim, transcendentals=0),
         compiler_params=pltpu.CompilerParams(

time: 68.2 us -> 68.9 us (1.010)
  Pallas kernels: 67.5 us -> 68.2 us
where the time goes in v7:
time: 68.9 us; the launch traced here: 68.8 us
  Pallas kernels  68.2 us (99%)
    pallas_call x1, Pallas kernels, kernel_step(): make_kernel(n_dp, n_zero, mats, rows, dim)(grad_parts, momentum)  63.4 us
    pallas_call x1, Pallas kernels, kernel_step(): return make_finish(n_zero, mats, rows, dim)(owner_table, nm, update)  4.79 us

profile of v7, /device:TPU:0, one launch (start us, length us, event | category | flops | bytes accessed | tf_op | source)
XLA Modules:
  0.0 68.8 jit_solution(12219280139424442746)
XLA Ops:
  0.6 63.4 %shard_map.58 = (bf16[3,176,1024]{2,1,0:T(8,128)(2,1)}, bf16[3,704,1024]{2,1,0:T(8,128)(2,1)}) custom-call(bf16[1,3,176,1024]{3,2,1,0:T(8,128)(2,1)} %grad.1, f32[3,176,1024]{2,1,0:T(8,128)} %momentum.1), custom_call_target="tpu_custom_call" | custom-call | flops 8183611392 | bytes 8650752 | tf_op jit(solution)/shard_map/pallas_call | solution.py:483
  64.0 4.8 %shard_map.59 = (f32[3,176,1024]{2,1,0:T(8,128)}, bf16[3,176,1024]{2,1,0:T(8,128)(2,1)}, bf16[1,704,1024]{2,1,0:T(8,128)(2,1)}) custom-call(s32[3]{0:T(128)} %table.1, bf16[3,176,1024]{2,1,0:T(8,128)(2,1)} %get-tuple-element.5.nm, bf16[3,704,1024]{2,1,0:T(8,128)(2,1)} %get-tuple-element.6.update), custom_call_target="tpu_custom_call" | custom-call | bytes 8650752 | tf_op jit(solution)/shard_map/pallas_call | solution.py:484

commit v8 on v7

--- a/solution.py
+++ b/solution.py
@@ -194,10 +194,10 @@
             for r in range(n_line - 1):
                 total = total + parts[j, r].astype(jnp.float32)
             x[j, d, row(o), :] = (MOMENTUM_DECAY * mom[j] + total).astype(jnp.bfloat16)
+            for r in range(1, n_line):
+                s1(j, r).start()
             s3(j, 0, 0).start()
             s2(j, 0).start()
-            for r in range(1, n_line):
-                s1(j, r).start()
 
         def phase_b(j):
             for r in range(1, n_line):
@@ -312,24 +312,24 @@
         phase_a(2)
         phase_b(1)
         phase_d(0)
+        phase_c(1)
+        phase_b(2)
         phase_e(0)
         gram_op(0, 0)
-        phase_c(1)
-        phase_b(2)
-        apply_op(0, 0)
         phase_c(2)
         phase_d(1)
+        apply_op(0, 0)
         phase_e(1)
         gram_op(1, 0)
+        phase_d(2)
         gram_op(0, 1)
-        phase_d(2)
         apply_op(1, 0)
-        apply_op(0, 1)
         phase_e(2)
         gram_op(2, 0)
+        apply_op(0, 1)
         gram_op(1, 1)
+        apply_op(2, 0)
         finish(0)
-        apply_op(2, 0)
         apply_op(1, 1)
         gram_op(2, 1)
         finish(1)

time: 68.9 us -> 68 us (0.987)
  Pallas kernels: 68.2 us -> 67.3 us
    pallas_call x1, Pallas kernels: 63.4 us -> 62.5 us  [kernel_step(): make_kernel(n_dp, n_zero, mats, rows, dim)(grad_parts, momentum)]
where the time goes in v8:
time: 68 us; the launch traced here: 67.9 us
  Pallas kernels  67.3 us (99%)
    pallas_call x1, Pallas kernels, kernel_step(): make_kernel(n_dp, n_zero, mats, rows, dim)(grad_parts, momentum)  62.5 us
    pallas_call x1, Pallas kernels, kernel_step(): return make_finish(n_zero, mats, rows, dim)(owner_table, nm, update)  4.74 us

profile of v8, /device:TPU:0, one launch (start us, length us, event | category | flops | bytes accessed | tf_op | source)
XLA Modules:
  0.0 67.9 jit_solution(7677809101153133031)
XLA Ops:
  0.6 62.5 %shard_map.58 = (bf16[3,176,1024]{2,1,0:T(8,128)(2,1)}, bf16[3,704,1024]{2,1,0:T(8,128)(2,1)}) custom-call(bf16[1,3,176,1024]{3,2,1,0:T(8,128)(2,1)} %grad.1, f32[3,176,1024]{2,1,0:T(8,128)} %momentum.1), custom_call_target="tpu_custom_call" | custom-call | flops 8183611392 | bytes 8650752 | tf_op jit(solution)/shard_map/pallas_call | solution.py:483
  63.2 4.7 %shard_map.59 = (f32[3,176,1024]{2,1,0:T(8,128)}, bf16[3,176,1024]{2,1,0:T(8,128)(2,1)}, bf16[1,704,1024]{2,1,0:T(8,128)(2,1)}) custom-call(s32[3]{0:T(128)} %table.1, bf16[3,176,1024]{2,1,0:T(8,128)(2,1)} %get-tuple-element.5.nm, bf16[3,704,1024]{2,1,0:T(8,128)(2,1)} %get-tuple-element.6.update), custom_call_target="tpu_custom_call" | custom-call | bytes 8650752 | tf_op jit(solution)/shard_map/pallas_call | solution.py:484
